TPU v7x, 512 devices: a whole 4x8x8 slice. The times are simulated.
512 devices in a mesh: dp: 16 (over y, core), expert: 32 (over z, x).
Axes of the slice: x: 4, y: 8, z: 8, core: 2. Of those that a mesh axis runs over, the one named last changes fastest.
Arguments:
- stream_q: bfloat16 [4096, 4096], P('dp', 'expert'), may hold values from -6 to 6
- stream_k: bfloat16 [4096, 4096], P('dp', 'expert'), may hold values from -6 to 6
- stream_v: bfloat16 [4096, 4096], P('dp', 'expert'), may hold values from -6 to 6
- conv_taps: float32 [3, 3, 4096], P(None, None, 'expert'), may hold values from -14 to 14
- norm_gain: bfloat16 [4096], P('expert'), may hold values from 0.3984375 to 1.59375
- slot_token: int32 [16, 384], P('dp'), may hold values from 0 to 256, as said below
- expert_count: int32 [16, 2], P('dp'), may hold values from 0 to 256, as said below
- route_prob: float32 [4096], P('dp'), may hold values from 0.25 to 1
- w_proj: bfloat16 [4096, 2, 8192], P('dp', None, 'expert'), may hold values from -0.09375 to 0.09375
- grad_out: bfloat16 [4096, 8192], P('dp', 'expert'), may hold values from -0.75 to 0.75
Outputs:
- activation: bfloat16 [4096, 8192], P('dp', 'expert')
- weight_grad: float32 [4096, 2, 8192], P('dp', None, 'expert')
Inputs may be any that keep to these rules, and one draw needn't show every extreme that they name: `slot_token`: for each index of dp the slots hold its 256 local token numbers, each exactly once, grouped by expert in expert order; each group starts at a multiple of 128 and is padded with the value 256 up to a multiple of 128; all slots after the last group hold 256. `expert_count`: the size of each expert's group in slot_token, before padding; each row sums to 256.
All inputs are finite; a program needn't handle non-finite values.
Results may differ from a plain program's by a relative error of at most 0.023.
Values may be sent and summed in bfloat16 or wider, within the bound.
No kernel may reach another device: no remote copies, remote signals or barrier semaphores. Data moves between devices by JAX's collectives and lax.ppermute only.
A program may use at most 64 MiB of HBM per device.

v0:
```python
import jax
import jax.numpy as jnp
from jax import lax
from jax.sharding import PartitionSpec as P

D = 4096
BLOCK = 128
epsilon = 1e-06


def from_behind(value, axis, steps):
    count = lax.axis_size(axis)
    leading, last = (max(0, -steps), min(count, count - steps))
    return lax.ppermute(value, axis, [(source, source + steps) for source in range(leading, last)])


def block_owner(counts, num_blocks):
    padded = (counts + BLOCK - 1) // BLOCK * BLOCK
    ends = jnp.cumsum(padded)
    starts = jnp.arange(num_blocks, dtype=jnp.int32) * BLOCK
    owner = jnp.sum((starts[:, None] >= ends[None, :]).astype(jnp.int32), axis=1)
    return jnp.minimum(owner, counts.shape[0] - 1)


def on_device(
    stream_q,
    stream_k,
    stream_v,
    conv_taps,
    norm_gain,
    slot_token,
    expert_count,
    route_prob,
    w_proj,
    grad_out,
):
    stacked = jnp.stack([stream_q, stream_k, stream_v])
    before = from_behind(stacked[:, -2:, :], "dp", 1)
    extended = jnp.concatenate([before, stacked], axis=1).astype(jnp.float32)
    convolved = (
        conv_taps[:, 0, None, :] * extended[:, 2:]
        + conv_taps[:, 1, None, :] * extended[:, 1:-1]
        + conv_taps[:, 2, None, :] * extended[:, :-2]
    )
    mixed = (convolved[0] * convolved[1] * convolved[2]).astype(jnp.bfloat16)
    mixed_f = mixed.astype(jnp.float32)
    total = lax.psum(jnp.sum(mixed_f * mixed_f, axis=1), "expert")
    inv_rms = lax.rsqrt(total / D + epsilon)
    normed = (mixed_f * inv_rms[:, None] * norm_gain.astype(jnp.float32)).astype(jnp.bfloat16)
    gathered = lax.all_gather(normed, "expert", axis=1, tiled=True)
    tok_count = gathered.shape[0]
    slots = slot_token[0]
    num_blocks = slots.shape[0] // BLOCK
    owner = block_owner(expert_count[0], num_blocks)
    padded_rows = jnp.concatenate(
        [gathered, jnp.zeros((1, gathered.shape[1]), jnp.bfloat16)], axis=0
    )
    x_blocks = padded_rows[slots].reshape(num_blocks, BLOCK, gathered.shape[1])
    hid_local = w_proj.shape[2]
    experts_here = w_proj.shape[1]
    selector = (owner[:, None] == jnp.arange(experts_here, dtype=jnp.int32)[None, :]).astype(
        jnp.bfloat16
    )
    columns = x_blocks
    chosen_w = jnp.einsum(
        "neh,be->bnh",
        lax.all_gather(w_proj, "dp", axis=0, tiled=True),
        selector,
        preferred_element_type=jnp.float32,
    ).astype(jnp.bfloat16)
    pre_act = jnp.einsum("brn,bnh->brh", columns, chosen_w, preferred_element_type=jnp.float32)
    pre_act = pre_act.reshape(num_blocks * BLOCK, hid_local)
    slot_prob = jnp.concatenate([route_prob, jnp.zeros((1,), jnp.float32)])[slots][:, None]
    sigmoid_z = jax.nn.sigmoid(pre_act)
    hidden = (slot_prob * pre_act * sigmoid_z).astype(jnp.bfloat16)
    activation = (
        jnp.zeros((tok_count + 1, hid_local), jnp.bfloat16).at[slots].set(hidden)[:tok_count]
    )
    slot_grad = jnp.concatenate([grad_out, jnp.zeros((1, hid_local), jnp.bfloat16)], axis=0)[
        slots
    ].astype(jnp.float32)
    grad_pre = (slot_grad * slot_prob * sigmoid_z * (1.0 + pre_act * (1.0 - sigmoid_z))).astype(
        jnp.bfloat16
    )
    grad_blocks = grad_pre.reshape(num_blocks, BLOCK, hid_local)
    masked_grad = grad_blocks[None, :, :, :] * selector.T[:, :, None, None]
    columns = x_blocks
    weight_grad = lax.psum_scatter(
        jnp.einsum(
            "brd,ebrh->deh", columns, masked_grad, preferred_element_type=jnp.float32
        ).astype(jnp.bfloat16),
        "dp",
        scatter_dimension=0,
        tiled=True,
    ).astype(jnp.float32)
    return (activation, weight_grad)


def solution(mesh):
    placed = (
        P("dp", "expert"),
        P("dp", "expert"),
        P("dp", "expert"),
        P(None, None, "expert"),
        P("expert"),
        P("dp", None),
        P("dp", None),
        P("dp"),
        P("dp", None, "expert"),
        P("dp", "expert"),
    )
    return jax.shard_map(
        on_device,
        mesh=mesh,
        in_specs=placed,
        out_specs=(P("dp", "expert"), P("dp", None, "expert")),
        check_vma=False,
    )
```

profile of v0, /device:TPU:29, one launch (start us, length us, event | category | flops | bytes accessed | tf_op | source)
XLA Modules:
  0.0 303.6 jit_solution(1994741817525698117)
XLA Ops:
  7.2 0.0 copy-start.2
  7.2 0.0 copy-start.3
  7.2 0.0 all-gather.3.cloned.1.call-start
  7.2 0.7 pad_maximum_fusion.1
  8.0 5.0 %collective-permute-start = (bf16[3,2,128]{2,1,0:T(2,128)(2,1)S(1)}, bf16[3,2,128]{2,1,0:T(2,128)(2,1)S(1)}, u32[]{:S(2)}, u32[]{:S(2)}) collective-permute-start(bf16[3,2,128]{2,1,0:T(2,128)(2,1)S(1)} %pad_maximum_fusion.1), channel_id=1, source_target_pairs={{0,32},{32,64},{64,96},{96,128},{128,160},{160,192},{192,224},{224... | collective-permute-start | bytes 4616 | tf_op jit(solution)/shard_map/ppermute | solution.py:14
  12.9 0.8 fusion.29
  13.8 0.7 convert_element_type.59
  14.4 0.0 collective-permute-done
  14.4 0.9 maximum_convert_fusion
  15.4 0.1 fusion.2
  15.5 0.1 fusion.15
  15.6 62.6 %psum.7 = f32[256]{0:T(256)S(1)} all-reduce(f32[256]{0:T(256)S(1)} %get-tuple-element.10), channel_id=1, replica_groups=mesh['dp'=16,'expert'=32] {'expert'}, use_global_device_ids=true, to_apply=%region_1.0 | all-reduce | flops 256 | bytes 2048 | tf_op jit(solution)/shard_map/psum | solution.py:47
  78.2 0.7 fusion.17
  79.0 0.0 all-gather.3.cloned.1.call-update
  79.0 0.0 all-gather.5.cloned.1.call-start
  79.0 0.7 all-gather.5.cloned.1.call-update
  79.7 0.0 reduce-scatter.2.cloned.1.call-start
  79.8 0.7 pad_maximum_fusion
  80.5 0.7 fusion.24
  81.2 2.8 gather_fusion
  84.0 0.0 copy-done.2
  84.0 2.6 gather_fusion.2
  86.6 0.0 copy-done.3
  86.6 0.2 reduce-window.8
  86.8 0.1 fusion.25
  86.9 81.5 %all-gather.3.cloned.1.call-done = bf16[256,4096]{1,0:T(8,128)(2,1)} async-done(((bf16[256,128]{1,0:T(8,128)(2,1)}), bf16[256,4096]{1,0:T(8,128)(2,1)}) %all-gather.3.cloned.1.call-update) | async-done | bytes 2097168 | tf_op jit(solution)/shard_map/all_gather | solution.py:50
  168.4 1.8 concatenate.14
  170.1 4.1 %gather_fusion.1 = bf16[384,4096]{1,0:T(8,128)(2,1)} fusion(bf16[257,4096]{1,0:T(8,128)(2,1)S(1)} %concatenate.14, s32[1024]{0:T(1024)S(1)} %pad_clamp_fusion), kind=kCustom, calls=%fused_computation.1 | custom fusion | bytes 6292992 | tf_op jit(solution)/shard_map/gather | solution.py:58
  174.2 0.0 copy-start
  174.2 42.7 %all-gather.5.cloned.1.call-done = bf16[4096,2,256]{2,1,0:T(2,128)(2,1)} async-done(((bf16[256,2,256]{2,1,0:T(2,128)(2,1)}), bf16[4096,2,256]{2,1,0:T(2,128)(2,1)}) %all-gather.5.cloned.1.call-update) | async-done | bytes 4194320 | tf_op jit(solution)/shard_map/all_gather | solution.py:67
  217.0 0.0 copy-start.1
  217.0 7.5 %convolution_convert_fusion = bf16[3,4096,256]{2,0,1:T(4,128)(2,1)S(1)} fusion(bf16[4096,2,256]{2,1,0:T(2,128)(2,1)} %all-gather.5.cloned.1.call-done, s32[3]{0:T(128)S(1)} %broadcast_minimum_fusion), kind=kOutput, calls=%fused_computation.5 | convolution fusion | flops 15728646 | bytes 10485772 | tf_op jit(solution)/shard_map/neh,be->bnh/dot_general | solution.py:65
  224.4 0.0 copy-done
  224.5 0.0 copy-done.1
  224.5 1.3 fusion.6
  225.8 4.4 %bitcast_convert_fusion = bf16[4096,2,256]{2,0,1:T(8,128)(2,1)} fusion(bf16[3,128,4096,1]{2,1,0,3:T(8,128)(2,1)S(1)} %bitcast.50, bf16[2,3]{1,0:T(2,128)(2,1)S(1)} %compare_convert_fusion, bf16[3,128,256]{2,1,0:T(8,128)(2,1)S(1)} %get-tuple-element.15), kind=kOutput, calls=%fused_computation.4 | convolution fusion | flops 1613496320 | bytes 7536652 | tf_op jit(solution)/shard_map/brd,ebrh->deh/dot_general | solution.py:89
  230.1 0.0 reduce-scatter.2.cloned.1.call-update
  230.2 0.1 fusion.8
  230.3 1.9 scatter_custom_fusion
  232.2 0.7 slice.56
  232.8 62.2 %reduce-scatter.2.cloned.1.call-done = bf16[256,2,256]{2,0,1:T(8,128)(2,1)} async-done(((bf16[4096,2,256]{2,0,1:T(8,128)(2,1)}), bf16[256,2,256]{2,0,1:T(8,128)(2,1)}) %reduce-scatter.2.cloned.1.call-update) | async-done | bytes 262160 | tf_op jit(solution)/shard_map/reduce_scatter | solution.py:88
  295.1 2.0 copy.21
  (9 shorter events, 0.1 us)
Async XLA Ops:
  7.2 76.8 %copy-start.2 = (bf16[256,256]{1,0:T(8,128)(2,1)S(1)}, bf16[256,256]{1,0:T(8,128)(2,1)}, u32[]{:S(2)}) copy-start(bf16[256,256]{1,0:T(8,128)(2,1)} %param.19) | copy-start | bytes 393220
  7.2 79.4 %copy-start.3 = (s32[1,2]{1,0:T(1,128)S(1)}, s32[1,2]{1,0:T(1,128)}, u32[]{:S(2)}) copy-start(s32[1,2]{1,0:T(1,128)} %param.16) | copy-start | bytes 28
  7.2 161.2 %all-gather.3.cloned.1.call-start = ((), (), s32[]{:S(2)}) async-start(), calls=%async_computation.1 | async-start | bytes 2162688 | tf_op jit(solution)/shard_map/all_gather | solution.py:50
  8.0 6.5 %collective-permute-start = (bf16[3,2,128]{2,1,0:T(2,128)(2,1)S(1)}, bf16[3,2,128]{2,1,0:T(2,128)(2,1)S(1)}, u32[]{:S(2)}, u32[]{:S(2)}) collective-permute-start(bf16[3,2,128]{2,1,0:T(2,128)(2,1)S(1)} %pad_maximum_fusion.1), channel_id=1, source_target_pairs={{0,32},{32,64},{64,96},{96,128},{128,160},{160,192},{192,224},{224... | collective-permute-start | bytes 4616 | tf_op jit(solution)/shard_map/ppermute | solution.py:14
  79.0 138.0 %all-gather.5.cloned.1.call-start = ((), (), s32[]{:S(2)}) async-start(), calls=%async_computation.2 | async-start | bytes 4456448 | tf_op jit(solution)/shard_map/all_gather | solution.py:67
  79.7 215.3 %reduce-scatter.2.cloned.1.call-start = ((), (), s32[]{:S(2)}) async-start(), calls=%async_computation.3 | async-start | bytes 4456448 | tf_op jit(solution)/shard_map/reduce_scatter | solution.py:88
  174.2 50.2 %copy-start = (bf16[384,4096]{1,0:T(8,128)(2,1)S(1)}, bf16[384,4096]{1,0:T(8,128)(2,1)}, u32[]{:S(2)}) copy-start(bf16[384,4096]{1,0:T(8,128)(2,1)} %gather_fusion.1) | copy-start | bytes 9437188
  217.0 7.5 %copy-start.1 = (bf16[384,256]{1,0:T(8,128)(2,1)S(1)}, bf16[384,256]{1,0:T(8,128)(2,1)}, u32[]{:S(2)}) copy-start(bf16[384,256]{1,0:T(8,128)(2,1)} %gather_fusion.2) | copy-start | bytes 589828
Sparse Core Ops, SparseCore 0:
  79.1 89.2 all-gather.2
  170.5 46.4 all-gather.4
  230.3 64.7 reduce-scatter.1
where the time goes:
time: 304 us
  waiting for transfers between devices  187 us (62%)
  blocking collectives  62.6 us (21%)
  local copies, waits for them, and re-layouts  16.6 us (5%)
  between operations  13.9 us (5%)
  matrix products  13.1 us (4%)
  other arithmetic  5.15 us (2%)
  starting transfers between devices  5.08 us (2%)
    all_gather x1, waiting for transfers between devices, on_device(): gathered = lax.all_gather(normed, 'expert', axis=1, tiled=True)  81.5 us
    psum x1, blocking collectives, on_device(): total = lax.psum(jnp.sum(mixed_f * mixed_f, axis=1), 'expert')  62.6 us
    reduce_scatter x1, waiting for transfers between devices, on_device(): lax.psum_scatter(jnp.einsum('brd,ebrh->deh', columns, masked_grad, prefer...  62.2 us
    all_gather x1, waiting for transfers between devices, on_device(): lax.all_gather(w_proj, 'dp', axis=0, tiled=True)  42.7 us
    dot_general x1, matrix products, on_device(): jnp.einsum('neh,be->bnh', lax.all_gather(w_proj, 'dp', axis=0, tiled=True...  7.48 us
  transfers between devices with their start and end apart: 4, of which 3 were waited for; matrix products, arithmetic and copies ran while one was open for 6% of the time, Pallas kernels for 0%

commit v1 on v0

--- a/solution.py
+++ b/solution.py
@@ -47,7 +47,8 @@
     total = lax.psum(jnp.sum(mixed_f * mixed_f, axis=1), "expert")
     inv_rms = lax.rsqrt(total / D + epsilon)
     normed = (mixed_f * inv_rms[:, None] * norm_gain.astype(jnp.float32)).astype(jnp.bfloat16)
-    gathered = lax.all_gather(normed, "expert", axis=1, tiled=True)
+    copies = jnp.concatenate([normed] * lax.axis_size("expert"), axis=1)
+    gathered = lax.all_to_all(copies, "expert", 1, 1, tiled=True)
     tok_count = gathered.shape[0]
     slots = slot_token[0]
     num_blocks = slots.shape[0] // BLOCK

time: 304 us -> 227 us (0.75)
  the two profiles are of different devices: /device:TPU:29 before, /device:TPU:31 now
where the time goes in v1:
time: 227 us
  waiting for transfers between devices  103 us (45%)
  blocking collectives  59.2 us (26%)
  local copies, waits for them, and re-layouts  17.2 us (8%)
  starting transfers between devices  16.5 us (7%)
  between operations  14.2 us (6%)
  matrix products  13.3 us (6%)
  other arithmetic  3.14 us (1%)
    reduce_scatter x1, waiting for transfers between devices, on_device(): lax.psum_scatter(jnp.einsum('brd,ebrh->deh', columns, masked_grad, prefer...  71.9 us
    psum x1, blocking collectives, on_device(): total = lax.psum(jnp.sum(mixed_f * mixed_f, axis=1), 'expert')  59.2 us
    all_to_all x1, waiting for transfers between devices, on_device(): gathered = lax.all_to_all(copies, 'expert', 1, 1, tiled=True)  30.7 us
    all_to_all x1, starting transfers between devices, on_device(): gathered = lax.all_to_all(copies, 'expert', 1, 1, tiled=True)  11.5 us
    dot_general x1, matrix products, on_device(): jnp.einsum('neh,be->bnh', lax.all_gather(w_proj, 'dp', axis=0, tiled=True...  7.6 us
    ppermute x1, starting transfers between devices, from_behind(): lax.ppermute(value, axis, [(source, source + steps) for source in range(l...  4.96 us
  transfers between devices with their start and end apart: 4, of which 2 were waited for; matrix products, arithmetic and copies ran while one was open for 8% of the time, Pallas kernels for 0%

profile of v1, /device:TPU:31, one launch (start us, length us, event | category | flops | bytes accessed | tf_op | source)
XLA Modules:
  0.0 226.8 jit_solution(937960029635959912)
XLA Ops:
  7.2 0.0 all-gather.2.cloned.1.call-start
  7.2 0.7 all-gather.2.cloned.1.call-update
  7.9 0.7 pad_maximum_fusion.1
  8.6 5.0 %collective-permute-start = (bf16[3,2,128]{2,1,0:T(2,128)(2,1)S(1)}, bf16[3,2,128]{2,1,0:T(2,128)(2,1)S(1)}, u32[]{:S(2)}, u32[]{:S(2)}) collective-permute-start(bf16[3,2,128]{2,1,0:T(2,128)(2,1)S(1)} %pad_maximum_fusion.1), channel_id=1, source_target_pairs={{0,32},{32,64},{64,96},{96,128},{128,160},{160,192},{192,224},{224... | collective-permute-start | bytes 4616 | tf_op jit(solution)/shard_map/ppermute | solution.py:14
  13.6 0.8 fusion.29
  14.4 0.7 convert_element_type.164
  15.1 0.0 collective-permute-done
  15.1 0.9 maximum_convert_fusion
  16.0 0.1 fusion.2
  16.2 0.1 fusion.15
  16.3 59.2 %psum.7 = f32[256]{0:T(256)S(1)} all-reduce(f32[256]{0:T(256)S(1)} %get-tuple-element.10), channel_id=1, replica_groups=mesh['dp'=16,'expert'=32] {'expert'}, use_global_device_ids=true, to_apply=%region_1.0 | all-reduce | flops 256 | bytes 2048 | tf_op jit(solution)/shard_map/psum | solution.py:47
  75.5 0.1 fusion.17
  75.6 0.0 copy-start.4
  75.6 0.0 copy-start.3
  75.7 1.8 concatenate.18
  77.5 0.0 copy-start.2
  77.5 0.0 copy-start.5
  77.5 11.5 %all-to-all-start = ((bf16[256,32,128]{2,0,1:T(8,128)(2,1)}), bf16[256,32,128]{2,0,1:T(8,128)(2,1)S(1)}, u32[]{:S(2)}, u32[]{:S(2)}) async-start(bf16[256,32,128]{2,0,1:T(8,128)(2,1)} %concatenate.18), calls=%async_computation | async-start | bytes 4194304 | tf_op jit(solution)/shard_map/all_to_all | solution.py:51
  88.9 0.0 reduce-scatter.2.cloned.1.call-start
  89.0 0.0 copy-done.4
  89.0 0.0 copy-done.3
  89.1 2.8 %gather_fusion = f32[384]{0:T(512)S(1)} fusion(f32[257]{0:T(512)S(1)} %pad_maximum_fusion, s32[1024]{0:T(1024)S(1)} %pad_clamp_fusion), kind=kCustom, calls=%fused_computation | custom fusion | bytes 4608 | tf_op jit(solution)/shard_map/gather | solution.py:74
  91.9 0.0 copy-done.2
  91.9 2.6 %gather_fusion.2 = bf16[384,256]{1,0:T(8,128)(2,1)} fusion(bf16[257,256]{1,0:T(8,128)(2,1)S(1)} %concatenate.20, s32[1024]{0:T(1024)S(1)} %pad_clamp_fusion), kind=kCustom, calls=%fused_computation.2 | custom fusion | bytes 394752 | tf_op jit(solution)/shard_map/gather | solution.py:80
  94.5 0.0 copy-done.5
  94.5 0.2 reduce-window.8
  94.7 0.1 fusion.25
  94.8 30.7 %all-to-all-done = bf16[256,32,128]{2,0,1:T(8,128)(2,1)S(1)} async-done(((bf16[256,32,128]{2,0,1:T(8,128)(2,1)}), bf16[256,32,128]{2,0,1:T(8,128)(2,1)S(1)}, u32[]{:S(2)}, u32[]{:S(2)}) %all-to-all-start) | async-done | bytes 2097184 | tf_op jit(solution)/shard_map/all_to_all | solution.py:51
  125.5 0.3 copy_bitcast_fusion
  125.8 0.2 concatenate.19
  126.0 4.1 %gather_fusion.1 = bf16[384,4096]{1,0:T(8,128)(2,1)} fusion(bf16[257,4096]{1,0:T(8,128)(2,1)S(1)} %concatenate.19, s32[1024]{0:T(1024)S(1)} %pad_clamp_fusion), kind=kCustom, calls=%fused_computation.1 | custom fusion | bytes 6292992 | tf_op jit(solution)/shard_map/gather | solution.py:59
  130.1 0.0 copy-start
  130.1 0.0 all-gather.2.cloned.1.call-done
  130.1 0.0 copy-start.1
  130.1 7.6 %convolution_convert_fusion = bf16[3,4096,256]{2,0,1:T(4,128)(2,1)S(1)} fusion(bf16[4096,2,256]{2,1,0:T(2,128)(2,1)} %all-gather.2.cloned.1.call-done, s32[3]{0:T(128)S(1)} %broadcast_minimum_fusion), kind=kOutput, calls=%fused_computation.5 | convolution fusion | flops 15728646 | bytes 10485772 | tf_op jit(solution)/shard_map/neh,be->bnh/dot_general | solution.py:66
  137.7 0.0 copy-done
  137.7 0.0 copy-done.1
  137.7 1.3 fusion.6
  139.0 4.4 %bitcast_convert_fusion = bf16[4096,2,256]{2,0,1:T(8,128)(2,1)} fusion(bf16[3,128,4096,1]{2,1,0,3:T(8,128)(2,1)S(1)} %bitcast.55, bf16[2,3]{1,0:T(2,128)(2,1)S(1)} %compare_convert_fusion, bf16[3,128,256]{2,1,0:T(8,128)(2,1)S(1)} %get-tuple-element.15), kind=kOutput, calls=%fused_computation.4 | convolution fusion | flops 1613496320 | bytes 7536652 | tf_op jit(solution)/shard_map/brd,ebrh->deh/dot_general | solution.py:90
  143.4 0.0 reduce-scatter.2.cloned.1.call-update
  143.4 0.1 fusion.8
  143.6 1.9 scatter_custom_fusion
  145.4 0.7 slice.56
  146.1 71.9 %reduce-scatter.2.cloned.1.call-done = bf16[256,2,256]{2,0,1:T(8,128)(2,1)} async-done(((bf16[4096,2,256]{2,0,1:T(8,128)(2,1)}), bf16[256,2,256]{2,0,1:T(8,128)(2,1)}) %reduce-scatter.2.cloned.1.call-update) | async-done | bytes 262160 | tf_op jit(solution)/shard_map/reduce_scatter | solution.py:89
  218.0 2.0 copy.23
  (11 shorter events, 0.1 us)
Async XLA Ops:
  7.2 122.9 %all-gather.2.cloned.1.call-start = ((), (), s32[]{:S(2)}) async-start(), calls=%async_computation.2 | async-start | bytes 4456448 | tf_op jit(solution)/shard_map/all_gather | solution.py:68
  8.6 6.5 %collective-permute-start = (bf16[3,2,128]{2,1,0:T(2,128)(2,1)S(1)}, bf16[3,2,128]{2,1,0:T(2,128)(2,1)S(1)}, u32[]{:S(2)}, u32[]{:S(2)}) collective-permute-start(bf16[3,2,128]{2,1,0:T(2,128)(2,1)S(1)} %pad_maximum_fusion.1), channel_id=1, source_target_pairs={{0,32},{32,64},{64,96},{96,128},{128,160},{160,192},{192,224},{224... | collective-permute-start | bytes 4616 | tf_op jit(solution)/shard_map/ppermute | solution.py:14
  75.6 13.4 %copy-start.4 = (f32[256]{0:T(256)S(1)}, f32[256]{0:T(256)}, u32[]{:S(2)}) copy-start(f32[256]{0:T(256)} %param.17) | copy-start | bytes 3076
  75.6 13.4 %copy-start.3 = (s32[1,384]{1,0:T(1,128)S(1)}, s32[1,384]{1,0:T(1,128)}, u32[]{:S(2)}) copy-start(s32[1,384]{1,0:T(1,128)} %param.15) | copy-start | bytes 4612
  77.5 14.4 %copy-start.2 = (bf16[256,256]{1,0:T(8,128)(2,1)S(1)}, bf16[256,256]{1,0:T(8,128)(2,1)}, u32[]{:S(2)}) copy-start(bf16[256,256]{1,0:T(8,128)(2,1)} %param.19) | copy-start | bytes 393220
  77.5 17.0 %copy-start.5 = (s32[1,2]{1,0:T(1,128)S(1)}, s32[1,2]{1,0:T(1,128)}, u32[]{:S(2)}) copy-start(s32[1,2]{1,0:T(1,128)} %param.16) | copy-start | bytes 28
  77.5 48.0 %all-to-all-start = ((bf16[256,32,128]{2,0,1:T(8,128)(2,1)}), bf16[256,32,128]{2,0,1:T(8,128)(2,1)S(1)}, u32[]{:S(2)}, u32[]{:S(2)}) async-start(bf16[256,32,128]{2,0,1:T(8,128)(2,1)} %concatenate.18), calls=%async_computation | async-start | bytes 4194304 | tf_op jit(solution)/shard_map/all_to_all | solution.py:51
  88.9 129.0 %reduce-scatter.2.cloned.1.call-start = ((), (), s32[]{:S(2)}) async-start(), calls=%async_computation.3 | async-start | bytes 4456448 | tf_op jit(solution)/shard_map/reduce_scatter | solution.py:89
  130.1 7.6 %copy-start = (bf16[384,4096]{1,0:T(8,128)(2,1)S(1)}, bf16[384,4096]{1,0:T(8,128)(2,1)}, u32[]{:S(2)}) copy-start(bf16[384,4096]{1,0:T(8,128)(2,1)} %gather_fusion.1) | copy-start | bytes 9437188
  130.1 7.6 %copy-start.1 = (bf16[384,256]{1,0:T(8,128)(2,1)S(1)}, bf16[384,256]{1,0:T(8,128)(2,1)}, u32[]{:S(2)}) copy-start(bf16[384,256]{1,0:T(8,128)(2,1)} %gather_fusion.2) | copy-start | bytes 589828
Sparse Core Ops, SparseCore 0:
  10.1 48.7 all-gather.1
  143.5 74.4 reduce-scatter.1
